TPU v7x, 512 devices: a whole 4x8x8 slice. The times are simulated.
512 devices in a mesh: dp: 16 (over y, core), seq: 32 (over x, z).
Axes of the slice: x: 4, y: 8, z: 8, core: 2. Of those that a mesh axis runs over, the one named last changes fastest.
Arguments:
- queries: bfloat16 [65536, 8192], P(('dp', 'seq')), may hold values from -8 to 8
- keys: bfloat16 [65536, 1024], P(('dp', 'seq')), may hold values from -8 to 8
- values: bfloat16 [65536, 1024], P(('dp', 'seq')), may hold values from -6 to 6
- doc_ids: int32 [65536], P(('dp', 'seq')), may hold values from 0 to 511, never falling along the last dimension, each value on 1 to 512 neighbouring positions
Outputs:
- attended: bfloat16 [65536, 8192], P(('dp', 'seq'))
Inputs may be any that keep to these rules, and one draw needn't show every extreme that they name: `doc_ids`: document ids never fall along the tokens; each document is 1 to 512 consecutive tokens, and some document has exactly 512.
All inputs are finite; a program needn't handle non-finite values.
Results may differ from a plain program's by a relative error of at most 0.0031.
Values may be sent and summed in bfloat16 or wider, within the bound.
A program may use at most 64 MiB of HBM per device.

v0:
```python
import jax
import jax.numpy as jnp
from jax import lax
from jax.sharding import PartitionSpec as P

QUERY_HEADS = 64
KEY_VALUE_HEADS = 8
HEAD_SIZE = 128
LONGEST_DOCUMENT = 512
QBLOCK = 512


def from_behind(block, axis, distance):
    devices = range(lax.axis_size(axis))
    route = [(i - distance, i) for i in devices if i - distance in devices]
    return lax.ppermute(block, axis, route)


def attend_block(
    query_block, key_window, value_window, query_docs, key_docs, query_offset, key_offset
):
    query_rows = query_block.shape[0]
    key_rows = key_window.shape[0]
    score_scale = query_block.shape[2] ** (-0.5)
    scores = (
        jnp.einsum("qhd,kd->hqk", query_block, key_window, preferred_element_type=jnp.float32)
        * score_scale
    )
    query_pos = query_offset + jnp.arange(query_rows, dtype=jnp.int32)
    key_pos = key_offset + jnp.arange(key_rows, dtype=jnp.int32)
    allowed = (query_docs[:, None] == key_docs[None, :]) & (key_pos[None, :] <= query_pos[:, None])
    scores = jnp.where(allowed[None], scores, -jnp.inf)
    row_max = jnp.max(scores, axis=2, keepdims=True)
    weight = jnp.exp(scores - row_max)
    totals = jnp.sum(weight, axis=2, keepdims=True)
    mixed_out = jnp.einsum(
        "hqk,kd->qhd", weight.astype(jnp.bfloat16), value_window, preferred_element_type=jnp.float32
    )
    mixed_out = mixed_out / jnp.transpose(totals, (1, 0, 2))
    return mixed_out.astype(jnp.bfloat16).reshape(query_rows, -1)


def on_device(queries, keys, values, doc_ids):
    token_rows = queries.shape[0]
    sequence_count = lax.axis_size("seq")
    head_size = HEAD_SIZE
    stacked = jnp.stack(
        [
            keys.reshape(token_rows, KEY_VALUE_HEADS, head_size),
            values.reshape(token_rows, KEY_VALUE_HEADS, head_size),
        ],
        axis=2,
    )
    heads_here = QUERY_HEADS // sequence_count
    head_copies = sequence_count // KEY_VALUE_HEADS
    slab_rows = token_rows * sequence_count
    query_parts = queries.reshape(token_rows, sequence_count, heads_here * head_size)
    spread_pairs = jnp.repeat(stacked, head_copies, axis=1).reshape(
        token_rows, sequence_count, 2 * head_size
    )
    query_slab, pair_slab = (
        lax.all_to_all(query_parts, "seq", split_axis=1, concat_axis=0, tiled=True),
        lax.all_to_all(spread_pairs, "seq", split_axis=1, concat_axis=0, tiled=True),
    )
    slab_doc_ids = lax.all_gather(doc_ids, "seq", axis=0, tiled=True)
    pair_slab = pair_slab.reshape(slab_rows, 2 * head_size)
    rim_pairs, rim_docs = from_behind(
        (
            pair_slab[slab_rows - LONGEST_DOCUMENT :],
            slab_doc_ids[slab_rows - LONGEST_DOCUMENT :] + 1,
        ),
        "dp",
        1,
    )
    query_slab = query_slab.reshape(slab_rows, heads_here, head_size)
    pair_ext = jnp.concatenate([rim_pairs, pair_slab], axis=0)
    key_ext = pair_ext[:, :head_size]
    value_ext = pair_ext[:, head_size:]
    doc_ext = jnp.concatenate([rim_docs - 1, slab_doc_ids], axis=0)

    def one_block(block_index):
        offset = block_index * QBLOCK
        query_block = lax.dynamic_slice_in_dim(query_slab, offset, QBLOCK, 0)
        query_docs = lax.dynamic_slice_in_dim(doc_ext, offset + LONGEST_DOCUMENT, QBLOCK, 0)
        key_width = LONGEST_DOCUMENT + QBLOCK
        key_window = lax.dynamic_slice_in_dim(key_ext, offset, key_width, 0)
        value_window = lax.dynamic_slice_in_dim(value_ext, offset, key_width, 0)
        key_docs = lax.dynamic_slice_in_dim(doc_ext, offset, key_width, 0)
        return attend_block(
            query_block,
            key_window,
            value_window,
            query_docs,
            key_docs,
            offset + LONGEST_DOCUMENT,
            offset,
        )

    outputs = lax.map(one_block, jnp.arange(slab_rows // QBLOCK, dtype=jnp.int32))
    outputs = outputs.reshape(slab_rows, heads_here * head_size)
    return lax.all_to_all(outputs, "seq", split_axis=0, concat_axis=1, tiled=True)


def solution(mesh):
    in_specs = (
        P(("dp", "seq"), None),
        P(("dp", "seq"), None),
        P(("dp", "seq"), None),
        P(("dp", "seq")),
    )
    out_specs = P(("dp", "seq"), None)
    return jax.shard_map(
        on_device, mesh=mesh, in_specs=in_specs, out_specs=out_specs, check_vma=False
    )
```

profile of v0, /device:TPU:1, one launch (start us, length us, event | category | flops | bytes accessed | tf_op | source)
XLA Modules:
  0.0 308.7 jit_solution(10227974468638128346)
XLA Ops:
  0.0 1.0 copy.36
  1.0 1.0 copy.37
  2.6 1.9 broadcast_in_dim.45
  4.5 2.6 reshape_reshape.3
  7.1 13.7 %all-to-all-start = ((bf16[128,32,256]{2,0,1:T(8,128)(2,1)}), bf16[128,32,256]{2,0,1:T(8,128)(2,1)S(1)}, u32[]{:S(2)}, u32[]{:S(2)}) async-start(bf16[128,32,256]{2,0,1:T(8,128)(2,1)} %reshape_reshape.3), calls=%async_computation | async-start | bytes 4194304 | tf_op jit(solution)/shard_map/all_to_all | solution.py:63
  20.8 4.1 %copy.24 = bf16[128,8192]{0,1:T(8,128)(2,1)} copy(bf16[128,8192]{1,0:T(8,128)(2,1)} %param.6) | data formatting | bytes 4194304 | tf_op args[0]
  24.9 44.8 %all-to-all-done = bf16[128,32,256]{2,0,1:T(8,128)(2,1)S(1)} async-done(((bf16[128,32,256]{2,0,1:T(8,128)(2,1)}), bf16[128,32,256]{2,0,1:T(8,128)(2,1)S(1)}, u32[]{:S(2)}, u32[]{:S(2)}) %all-to-all-start) | async-done | bytes 2097184 | tf_op jit(solution)/shard_map/all_to_all | solution.py:63
  69.7 7.3 %all-to-all-start.1 = ((bf16[128,32,256]{0,2,1:T(8,128)(2,1)}), bf16[128,32,256]{0,2,1:T(8,128)(2,1)}, u32[]{:S(2)}, u32[]{:S(2)}) async-start(bf16[128,32,256]{0,2,1:T(8,128)(2,1)} %bitcast.87), calls=%async_computation.1 | async-start | bytes 4194304 | tf_op jit(solution)/shard_map/all_to_all | solution.py:62
  77.0 71.4 %all-gather = s32[32,1,128]{2,1,0:T(1,128)S(1)} all-gather(s32[1,1,128]{2,1,0:T(1,128)S(1)} %bitcast.100), channel_id=1, replica_groups=mesh['dp'=16,'seq'=32] {'seq'}, dimensions={0}, use_global_device_ids=true | all-gather | bytes 16896 | tf_op jit(solution)/shard_map/all_gather | solution.py:65
  148.4 11.5 %collective-permute-start.1 = (s32[512]{0:T(512)S(1)}, s32[512]{0:T(512)S(1)}, u32[]{:S(2)}, u32[]{:S(2)}) collective-permute-start(s32[512]{0:T(512)S(1)} %bitcast.99), channel_id=1, source_target_pairs={{0,32},{32,64},{64,96},{96,128},{128,160},{160,192},{192,224},{224... | collective-permute-start | bytes 6152 | tf_op jit(solution)/shard_map/ppermute | solution.py:16
  159.9 1.9 collective-permute-start
  162.5 4.2 %copy.25 = bf16[32,128,1,256]{1,0,3,2:T(8,128)(2,1)} copy(bf16[32,128,1,256]{1,3,0,2:T(8,128)(2,1)} %bitcast.19) | data formatting | bytes 4194304 | tf_op jit(solution)/shard_map/all_to_all | solution.py:62
  166.7 4.1 %reshape.89 = bf16[4096,2,128]{0,2,1:T(8,128)(2,1)} reshape(bf16[32,128,1,256]{1,0,3,2:T(8,128)(2,1)} %copy.25) | data formatting | bytes 4194304 | tf_op jit(solution)/shard_map/reshape | solution.py:75
  170.9 1.2 pad_maximum_fusion
  172.1 77.4 %while.12 = (s32[]{:T(128)}, bf16[8,512,256]{2,1,0:T(8,128)(2,1)}, s32[8]{0:T(128)S(1)}, bf16[4608,128]{1,0:T(8,128)(2,1)}, s32[4608]{0:T(1024)}, /*index=5*/bf1...) while((s32[]{:T(128)}, bf16[8,512,256]{2,1,0:T(8,128)(2,1)}, ...), condition=%wide.region_3.4_spmd, body=%wide.region_0.3_spmd.sunk | while | flops 550239744 | bytes 16829216 | solution.py:99
  174.9 0.8 compare_and_fusion.2
  175.7 1.9 fusion.33
  177.6 1.0 fusion.34
  178.6 2.3 fusion.35
  184.5 0.8 compare_and_fusion.2
  185.4 1.9 fusion.33
  187.3 1.0 fusion.34
  188.2 2.3 fusion.35
  194.2 0.8 compare_and_fusion.2
  195.1 1.9 fusion.33
  196.9 1.0 fusion.34
  197.9 2.3 fusion.35
  203.9 0.8 compare_and_fusion.2
  204.7 1.9 fusion.33
  206.6 1.0 fusion.34
  207.6 2.3 fusion.35
  213.6 0.8 compare_and_fusion.2
  214.4 1.9 fusion.33
  216.3 1.0 fusion.34
  217.3 2.3 fusion.35
  223.3 0.8 compare_and_fusion.2
  224.1 1.9 fusion.33
  226.0 1.0 fusion.34
  226.9 2.3 fusion.35
  233.8 1.9 fusion.33
  235.6 1.0 fusion.34
  236.6 2.3 fusion.35
  243.4 1.9 fusion.33
  245.3 1.0 fusion.34
  246.3 2.3 fusion.35
  249.5 52.3 %all_to_all.49 = bf16[32,128,256]{2,1,0:T(8,128)(2,1)S(1)} all-to-all(bf16[32,128,256]{2,1,0:T(8,128)(2,1)} %bitcast.91), channel_id=1, replica_groups=mesh['dp'=16,'seq'=32] {'seq'}, dimensions={0} | all-to-all | bytes 4194304 | tf_op jit(solution)/shard_map/all_to_all | solution.py:101
  301.8 2.8 copy.29
  304.6 4.1 %copy.30 = bf16[128,8192]{1,0:T(8,128)(2,1)} copy(bf16[128,8192]{0,1:T(8,128)(2,1)} %bitcast.89) | data formatting | bytes 4194304 | tf_op jit(solution)/shard_map/all_to_all | solution.py:101
  (71 shorter events, 26.9 us)
Async XLA Ops:
  7.1 62.6 %all-to-all-start = ((bf16[128,32,256]{2,0,1:T(8,128)(2,1)}), bf16[128,32,256]{2,0,1:T(8,128)(2,1)S(1)}, u32[]{:S(2)}, u32[]{:S(2)}) async-start(bf16[128,32,256]{2,0,1:T(8,128)(2,1)} %reshape_reshape.3), calls=%async_computation | async-start | bytes 4194304 | tf_op jit(solution)/shard_map/all_to_all | solution.py:63
  69.7 7.3 %copy-start = (s32[128]{0:T(128)S(1)}, s32[128]{0:T(128)}, u32[]{:S(2)}) copy-start(s32[128]{0:T(128)} %param.9) | copy-start | bytes 1540
  69.7 92.7 %all-to-all-start.1 = ((bf16[128,32,256]{0,2,1:T(8,128)(2,1)}), bf16[128,32,256]{0,2,1:T(8,128)(2,1)}, u32[]{:S(2)}, u32[]{:S(2)}) async-start(bf16[128,32,256]{0,2,1:T(8,128)(2,1)} %bitcast.87), calls=%async_computation.1 | async-start | bytes 4194304 | tf_op jit(solution)/shard_map/all_to_all | solution.py:62
  148.4 13.4 %collective-permute-start.1 = (s32[512]{0:T(512)S(1)}, s32[512]{0:T(512)S(1)}, u32[]{:S(2)}, u32[]{:S(2)}) collective-permute-start(s32[512]{0:T(512)S(1)} %bitcast.99), channel_id=1, source_target_pairs={{0,32},{32,64},{64,96},{96,128},{128,160},{160,192},{192,224},{224... | collective-permute-start | bytes 6152 | tf_op jit(solution)/shard_map/ppermute | solution.py:16
  159.9 11.0 %collective-permute-start = (bf16[512,256]{1,0:T(8,128)(2,1)S(1)}, bf16[512,256]{1,0:T(8,128)(2,1)S(1)}, u32[]{:S(2)}, u32[]{:S(2)}) collective-permute-start(bf16[512,256]{1,0:T(8,128)(2,1)S(1)} %bitcast.96), channel_id=1, source_target_pairs={{0,32},{32,64},{64,96},{96,128},{128,160},{160,192},{192,224},{224... | collective-permute-start | bytes 786440 | tf_op jit(solution)/shard_map/ppermute | solution.py:16
where the time goes:
time: 315 us; the launch traced here: 309 us
  blocking collectives  124 us (39%)
  local copies, waits for them, and re-layouts  50.3 us (16%)
  waiting for transfers between devices  44.8 us (14%)
  starting transfers between devices  34.4 us (11%)
  matrix products  33.5 us (11%)
  other arithmetic  16.3 us (5%)
  loops' own time  5.52 us (2%)
    all_gather x1, blocking collectives, on_device(): slab_doc_ids = lax.all_gather(doc_ids, 'seq', axis=0, tiled=True)  71.4 us
    all_to_all x1, blocking collectives, on_device(): lax.all_to_all(outputs, 'seq', split_axis=0, concat_axis=1, tiled=True)  52.3 us
    all_to_all x1, waiting for transfers between devices, on_device(): lax.all_to_all(spread_pairs, 'seq', split_axis=1, concat_axis=0, tiled=True)  44.8 us
    dot_general x8, matrix products, attend_block(): jnp.einsum('hqk,kd->qhd', weight.astype(jnp.bfloat16), value_window, pref...  18.6 us
    dot_general x8, matrix products, attend_block(): jnp.einsum('qhd,kd->hqk', query_block, key_window, preferred_element_type...  14.9 us
    all_to_all x1, starting transfers between devices, on_device(): lax.all_to_all(spread_pairs, 'seq', split_axis=1, concat_axis=0, tiled=True)  13.7 us
    ppermute x2, starting transfers between devices, from_behind(): return lax.ppermute(block, axis, route)  13.4 us
    reduce_sum x8, other arithmetic, attend_block(): totals = jnp.sum(weight, axis=2, keepdims=True)  7.87 us
  transfers between devices with their start and end apart: 4, of which 1 were waited for; matrix products, arithmetic and copies ran while one was open for 4% of the time, Pallas kernels for 0%

commit v1 on v0

v1 whole, which is shorter than its diff:
```python
import functools

import jax
import jax.numpy as jnp
from jax import lax
from jax.experimental import pallas as pl
from jax.experimental.pallas import tpu as pltpu
from jax.sharding import PartitionSpec as P

QUERY_HEADS = 64
KEY_VALUE_HEADS = 8
GROUP = QUERY_HEADS // KEY_VALUE_HEADS
HEAD_SIZE = 128
LONGEST_DOCUMENT = 512
MESH = pl.DeviceIdType.MESH
SCORE_SCALE = HEAD_SIZE**-0.5 * 1.4426950408889634

PLUS_HEADS = 5
REACH = 4
PLUS, MINUS = 0, 1


def arrivals(hop_us, latency_us, jump_hops):
    order = []
    for way, heads in ((PLUS, range(PLUS_HEADS)), (MINUS, range(PLUS_HEADS, KEY_VALUE_HEADS))):
        stages = range(1, REACH + 1) if way == PLUS else range(REACH + 1, 0, -1)
        clock, ready = 0.0, {head: 0.0 for head in heads}
        for distance in stages:
            for head in heads:
                clock = max(clock, ready[head]) + hop_us * (jump_hops if distance > REACH else 1)
                ready[head] = clock + latency_us
                order.append((ready[head], way, distance, head))
    return sorted(order)


def kernel(
    seq_size, device_count, order, queries, keys, values, docs, out,
    pairs, transit, query_rows, doc_rows, bias,
    local_sem, query_sem, send_sem, recv_sem, doc_send, doc_recv,
):
    me = lax.axis_index("dp") * seq_size + lax.axis_index("seq")

    def block_device(step):
        block = lax.rem(me + (step + device_count), device_count)
        return (block // seq_size, lax.rem(block, seq_size))

    right, left, ahead, behind = (block_device(s) for s in (1, -1, REACH + 1, -REACH - 1))
    barrier = pltpu.get_barrier_semaphore()
    for device in (right, left, behind):
        pl.semaphore_signal(barrier, inc=1, device_id=device, device_id_type=MESH)
    own = []
    for head in [*range(PLUS_HEADS, KEY_VALUE_HEADS), *range(PLUS_HEADS)]:
        for part, ref in enumerate((keys, values)):
            columns = ref.at[:, pl.ds(head * HEAD_SIZE, HEAD_SIZE)]
            own.append(pltpu.make_async_copy(columns, pairs.at[0, head, part], local_sem.at[head, part]))
            own[-1].start()
    query_copy = pltpu.make_async_copy(queries, query_rows, query_sem)
    query_copy.start()
    doc_rows[0] = jnp.broadcast_to(docs[...], doc_rows.shape[1:])
    for copy in own:
        copy.wait()
    pl.semaphore_wait(barrier, 3)

    def remote(source, target, sent, received, device):
        return pltpu.make_async_remote_copy(
            src_ref=source, dst_ref=target, send_sem=sent, recv_sem=received, device_id=device, device_id_type=MESH
        )

    copies = {}

    def send(way, distance, head):
        sems = (send_sem.at[distance - 1, head], recv_sem.at[distance - 1, head])
        if way == PLUS:
            copy = remote(pairs.at[distance - 1, head], pairs.at[distance, head], *sems, right)
        elif distance > REACH:
            copy = remote(pairs.at[0, head], transit.at[head - PLUS_HEADS], *sems, ahead)
        else:
            source = transit.at[head - PLUS_HEADS] if distance == REACH else pairs.at[distance + 1, head]
            copy = remote(source, pairs.at[distance, head], *sems, left)
        copy.start()
        copies[way, distance, head] = copy

    def doc_copy(distance):
        return remote(
            doc_rows.at[distance - 1], doc_rows.at[distance], doc_send.at[distance - 1], doc_recv.at[distance - 1], right
        )

    def attend(head):
        key_rows = jnp.concatenate([pairs[d, head, 0] for d in range(REACH + 1)], axis=0)
        value_rows = jnp.concatenate([pairs[d, head, 1] for d in range(REACH + 1)], axis=0)
        first = head * GROUP * HEAD_SIZE
        tokens = query_rows.shape[0]
        rows = jnp.concatenate(
            [query_rows[:, first + g * HEAD_SIZE : first + (g + 1) * HEAD_SIZE] for g in range(GROUP)], axis=0
        )
        scores = lax.dot_general(rows, key_rows, (((1,), (1,)), ((), ())), preferred_element_type=jnp.float32)
        scores = (scores * SCORE_SCALE).reshape(GROUP, tokens, -1) + bias[...][None]
        scores = scores.reshape(GROUP * tokens, -1)
        row_max = jnp.max(scores, axis=1, keepdims=True)
        weight = jnp.exp2(scores - row_max)
        totals = jnp.sum(weight, axis=1, keepdims=True)
        mixed = lax.dot_general(
            weight.astype(jnp.bfloat16), value_rows, (((1,), (0,)), ((), ())), preferred_element_type=jnp.float32
        )
        mixed = (mixed / totals).astype(jnp.bfloat16)
        for g in range(GROUP):
            out[:, first + g * HEAD_SIZE : first + (g + 1) * HEAD_SIZE] = mixed[g * tokens : (g + 1) * tokens]

    def fill_bias():
        tokens = query_rows.shape[0]
        query_docs = jnp.broadcast_to(docs[...], (tokens, tokens)).T
        for distance in range(REACH + 1):
            same = jnp.broadcast_to(doc_rows[distance, 0:1], (tokens, tokens)) == query_docs
            if distance == 0:
                row = lax.broadcasted_iota(jnp.int32, (tokens, tokens), 0)
                column = lax.broadcasted_iota(jnp.int32, (tokens, tokens), 1)
                same = same & (column <= row)
            else:
                same = same & (jnp.full((tokens, tokens), me, jnp.int32) >= distance)
            bias[:, distance * tokens : (distance + 1) * tokens] = jnp.where(same, 0.0, -jnp.inf)

    doc_copy(1).start()
    for head in range(PLUS_HEADS, KEY_VALUE_HEADS):
        send(MINUS, REACH + 1, head)
    for head in range(PLUS_HEADS):
        send(PLUS, 1, head)
    ready = []
    for position, (_, way, distance, head) in enumerate(order):
        if position % 3 == 2 and position // 3 < REACH:
            doc_distance = position // 3 + 1
            doc_copy(doc_distance).wait_recv()
            if doc_distance < REACH:
                doc_copy(doc_distance + 1).start()
            else:
                fill_bias()
                query_copy.wait()
        copies[way, distance, head].wait_recv()
        if way == PLUS and distance < REACH:
            send(PLUS, distance + 1, head)
        elif way == MINUS and distance > 1:
            send(MINUS, distance - 1, head)
        else:
            ready.append(head)
        if not any((w == PLUS and d < REACH) or (w == MINUS and d > 1) for _, w, d, _ in order[position + 1 :]):
            for done in ready:
                attend(done)
            ready = []
    for copy in copies.values():
        copy.wait_send()
    for distance in range(1, REACH + 1):
        doc_copy(distance).wait_send()


def on_device(seq_size, device_count, queries, keys, values, doc_ids):
    tokens = queries.shape[0]
    order = arrivals(1.38, 2.5, 1.5)
    pair = (tokens, HEAD_SIZE)
    links = (REACH + 1, KEY_VALUE_HEADS)
    return pl.pallas_call(
        functools.partial(kernel, seq_size, device_count, order),
        out_shape=jax.ShapeDtypeStruct(queries.shape, jnp.bfloat16),
        in_specs=[
            pl.BlockSpec(memory_space=pl.ANY),
            pl.BlockSpec(memory_space=pl.ANY),
            pl.BlockSpec(memory_space=pl.ANY),
            pl.BlockSpec(memory_space=pltpu.VMEM),
        ],
        out_specs=pl.BlockSpec(memory_space=pltpu.VMEM),
        scratch_shapes=[
            pltpu.VMEM((REACH + 1, KEY_VALUE_HEADS, 2, *pair), jnp.bfloat16),
            pltpu.VMEM((KEY_VALUE_HEADS - PLUS_HEADS, 2, *pair), jnp.bfloat16),
            pltpu.VMEM(queries.shape, jnp.bfloat16),
            pltpu.VMEM((REACH + 1, 8, tokens), jnp.int32),
            pltpu.VMEM((tokens, (REACH + 1) * tokens), jnp.float32),
            pltpu.SemaphoreType.DMA((KEY_VALUE_HEADS, 2)),
            pltpu.SemaphoreType.DMA,
            pltpu.SemaphoreType.DMA(links),
            pltpu.SemaphoreType.DMA(links),
            pltpu.SemaphoreType.DMA((REACH,)),
            pltpu.SemaphoreType.DMA((REACH,)),
        ],
        compiler_params=pltpu.CompilerParams(
            collective_id=0, has_side_effects=True, vmem_limit_bytes=60 * 1024 * 1024
        ),
    )(queries, keys, values, doc_ids.reshape(1, tokens))


def solution(mesh):
    seq_size = mesh.shape["seq"]
    spec = P(("dp", "seq"), None)
    return jax.shard_map(
        functools.partial(on_device, seq_size, mesh.shape["dp"] * seq_size),
        mesh=mesh,
        in_specs=(spec, spec, spec, P(("dp", "seq"))),
        out_specs=spec,
        check_vma=False,
    )
```

time: 315 us -> 64.4 us (0.20)
  the two profiles are of different devices: /device:TPU:1 before, /device:TPU:17 now
where the time goes in v1:
time: 64.4 us; the launch traced here: 64.2 us
  Pallas kernels  61.1 us (95%)
  local copies, waits for them, and re-layouts  3.1 us (5%)
    pallas_call x1, Pallas kernels, on_device(): pl.pallas_call(functools.partial(kernel, seq_size, device_count, order),...  61.1 us
    unnamed x1, local copies, waits for them, and re-layouts  3.1 us

profile of v1, /device:TPU:17, one launch (start us, length us, event | category | flops | bytes accessed | tf_op | source)
XLA Modules:
  0.0 64.2 jit_solution(9671746756844646399)
XLA Ops:
  0.0 61.1 %shard_map.46 = bf16[128,8192]{1,0:T(8,128)(2,1)} custom-call(bf16[128,8192]{1,0:T(8,128)(2,1)} %queries.1, bf16[128,1024]{1,0:T(8,128)(2,1)} %keys.1, bf16[128,1024]{1,0:T(8,128)(2,1)} %values.1, s32[1,128]{1,0:T(1,128)} %bitcast.1), custom_call_target="tpu_custom_call" | custom-call | tf_op jit(solution)/shard_map/pallas_call | solution.py:159
  61.1 3.1 %copy.6 = bf16[128,8192]{1,0:T(8,128)(2,1)} copy(bf16[128,8192]{1,0:T(8,128)(2,1)} %shard_map.46) | data formatting | bytes 4194304

commit v2 on v1

v2 whole, which is shorter than its diff:
```python
import functools

import jax
import jax.numpy as jnp
from jax import lax
from jax.experimental import pallas as pl
from jax.experimental.pallas import tpu as pltpu
from jax.sharding import PartitionSpec as P

QUERY_HEADS = 64
KEY_VALUE_HEADS = 8
GROUP = QUERY_HEADS // KEY_VALUE_HEADS
HEAD_SIZE = 128
LONGEST_DOCUMENT = 512
VMEM_BYTES = 40 << 20
HOLD = 1
LINE = 8
TIMES = (((3.9, 1.4), (7.0, 1.4, 4.2, 0.0), 3.0), ((3.9, 1.4), (7.0, 1.4, 4.2, 6.0), 3.0))


def own_first(dp, seq):
    return lax.rem(seq, LINE) < 3


MESH = pl.DeviceIdType.MESH
SCORE_SCALE = HEAD_SIZE**-0.5 * 1.4426950408889634

PLUS_HEADS = 5
REACH = 4
PLUS, MINUS = 0, 1
EARLY_BLOCKS = {PLUS: (1, 2), MINUS: (4, 3)}
LATE_BLOCKS = {PLUS: (3, 4), MINUS: (2, 1)}
EARLY_END = {(way, blocks[-1]) for way, blocks in EARLY_BLOCKS.items()}
LATE_END = {(way, blocks[-1]) for way, blocks in LATE_BLOCKS.items()}


def schedule(plus, minus, doc):
    steps = [(doc * distance, "doc", distance) for distance in range(1, REACH + 1)]
    for stage in range(REACH):
        for head in range(PLUS_HEADS):
            steps.append((plus[0] + plus[1] * (stage * PLUS_HEADS + head), "block", PLUS, stage + 1, head))
    for stage in range(REACH + 1):
        for index, head in enumerate(range(PLUS_HEADS, KEY_VALUE_HEADS)):
            steps.append((minus[0] + minus[1] * index + minus[2] * stage + (minus[3] if stage else 0.0), "block", MINUS, REACH + 1 - stage, head))
    return sorted(steps)


def kernel(
    seq_size, device_count, orders, queries, keys, values, docs, out,
    pairs, transit, query_rows, doc_rows, bias, top, total, partial,
    local_sem, query_sem, send_sem, recv_sem, doc_send, doc_recv,
):
    me = lax.axis_index("dp") * seq_size + lax.axis_index("seq")

    def block_device(step):
        block = lax.rem(me + (step + device_count), device_count)
        return (block // seq_size, lax.rem(block, seq_size))

    right, left, ahead, behind = (block_device(s) for s in (1, -1, REACH + 1, -REACH - 1))
    greet = (right, left, behind)
    barrier = pltpu.get_barrier_semaphore()
    for device in greet:
        pl.semaphore_signal(barrier, inc=1, device_id=device, device_id_type=MESH)
    own = []
    for head in [*range(PLUS_HEADS, KEY_VALUE_HEADS), *range(PLUS_HEADS)]:
        for part, ref in enumerate((keys, values)):
            columns = ref.at[:, pl.ds(head * HEAD_SIZE, HEAD_SIZE)]
            own.append(pltpu.make_async_copy(columns, pairs.at[0, head, part], local_sem.at[head, part]))
            own[-1].start()
    query_copy = pltpu.make_async_copy(queries, query_rows, query_sem)
    query_copy.start()
    doc_rows[0] = jnp.broadcast_to(docs[...], doc_rows.shape[1:])
    for copy in own:
        copy.wait()

    def remote(source, target, sent, received, device):
        return pltpu.make_async_remote_copy(
            src_ref=source, dst_ref=target, send_sem=sent, recv_sem=received, device_id=device, device_id_type=MESH
        )

    def block_copy(way, distance, head):
        sems = (send_sem.at[distance - 1, head], recv_sem.at[distance - 1, head])
        if way == PLUS:
            return remote(pairs.at[distance - 1, head], pairs.at[distance, head], *sems, right)
        if distance > REACH:
            return remote(pairs.at[0, head], transit.at[head - PLUS_HEADS], *sems, ahead)
        source = transit.at[head - PLUS_HEADS] if distance == REACH else pairs.at[distance + 1, head]
        return remote(source, pairs.at[distance, head], *sems, left)

    def doc_copy(distance):
        return remote(
            doc_rows.at[distance - 1], doc_rows.at[distance], doc_send.at[distance - 1], doc_recv.at[distance - 1], right
        )

    def attend(head, blocks, first, last):
        tokens = query_rows.shape[0]
        key_rows = jnp.concatenate([pairs[d, head, 0] for d in blocks], axis=0)
        value_rows = jnp.concatenate([pairs[d, head, 1] for d in blocks], axis=0)
        mask = jnp.concatenate([bias[d] for d in blocks], axis=0)
        columns = [pl.ds(pl.multiple_of((head * GROUP + g) * HEAD_SIZE, HEAD_SIZE), HEAD_SIZE) for g in range(GROUP)]
        rows = jnp.concatenate([query_rows[:, column] for column in columns], axis=0)
        scores = lax.dot_general(key_rows, rows, (((1,), (1,)), ((), ())), preferred_element_type=jnp.float32)
        scores = scores * SCORE_SCALE + jnp.concatenate([mask] * GROUP, axis=1)
        highest = jnp.max(scores, axis=0, keepdims=True)
        if not first:
            highest = jnp.maximum(highest, top[head])
        weight = jnp.exp2(scores - highest)
        sums = jnp.sum(weight, axis=0, keepdims=True)
        mixed = lax.dot_general(
            value_rows, weight.astype(jnp.bfloat16), (((0,), (0,)), ((), ())), preferred_element_type=jnp.float32
        )
        if not first:
            shrink = jnp.exp2(top[head] - highest)
            sums = sums + total[head] * shrink
            mixed = mixed + partial[head] * shrink
        if not last:
            top[head], total[head], partial[head] = highest, sums, mixed
            return
        mixed = mixed / sums
        for g, column in enumerate(columns):
            out[:, column] = mixed[:, g * tokens : (g + 1) * tokens].T.astype(jnp.bfloat16)

    def fill_bias(distance):
        tokens = query_rows.shape[0]
        square = (tokens, tokens)
        same = jnp.broadcast_to(doc_rows[distance, 0:1], square).T == jnp.broadcast_to(docs[...], square)
        if distance == 0:
            key, query = (lax.broadcasted_iota(jnp.int32, square, axis) for axis in (0, 1))
            same = same & (key <= query)
        else:
            same = same & (jnp.full(square, me, jnp.int32) >= distance)
        bias[distance] = jnp.where(same, 0.0, -jnp.inf)

    def attend_own():
        query_copy.wait()
        fill_bias(0)
        pl.loop(0, KEY_VALUE_HEADS)(lambda head: attend(head, (0,), True, False))

    early = own_first(lax.axis_index("dp"), lax.axis_index("seq"))
    pl.when(early)(attend_own)
    pl.semaphore_wait(barrier, len(greet))
    doc_copy(1).start()
    for head in range(PLUS_HEADS, KEY_VALUE_HEADS):
        block_copy(MINUS, REACH + 1, head).start()
    for head in range(PLUS_HEADS):
        block_copy(PLUS, 1, head).start()
    pl.when(jnp.logical_not(early))(attend_own)
    def follow(order):
        work, waiting = [], HOLD
        for step in order:
            if step[1] == "doc":
                doc_copy(step[2]).wait_recv()
                if step[2] < REACH:
                    doc_copy(step[2] + 1).start()
                fill_bias(step[2])
                waiting = 0 if step[2] == REACH else waiting
                continue
            way, distance, head = step[2:]
            block_copy(way, distance, head).wait_recv()
            if way == PLUS and distance < REACH:
                block_copy(PLUS, distance + 1, head).start()
            elif way == MINUS and distance > 1:
                block_copy(MINUS, distance - 1, head).start()
            if (way, distance) in EARLY_END:
                work.append((head, EARLY_BLOCKS[way], False, False))
            if (way, distance) in LATE_END:
                work.append((head, LATE_BLOCKS[way], False, True))
            if work and not waiting:
                attend(*work.pop(0))
        for item in work:
            attend(*item)

    first_half = lax.rem(lax.axis_index("seq"), LINE) < LINE // 2
    pl.when(first_half)(lambda: follow(orders[0]))
    pl.when(jnp.logical_not(first_half))(lambda: follow(orders[1]))
    for way, distance, head in (step[2:] for step in orders[0] if step[1] == "block"):
        block_copy(way, distance, head).wait_send()
    for distance in range(1, REACH + 1):
        doc_copy(distance).wait_send()


def on_device(seq_size, device_count, queries, keys, values, doc_ids):
    tokens = queries.shape[0]
    orders = [schedule(*times) for times in TIMES]
    pair = (tokens, HEAD_SIZE)
    links = (REACH + 1, KEY_VALUE_HEADS)
    return pl.pallas_call(
        functools.partial(kernel, seq_size, device_count, orders),
        out_shape=jax.ShapeDtypeStruct(queries.shape, jnp.bfloat16),
        in_specs=[
            pl.BlockSpec(memory_space=pltpu.HBM),
            pl.BlockSpec(memory_space=pltpu.HBM),
            pl.BlockSpec(memory_space=pltpu.HBM),
            pl.BlockSpec(memory_space=pltpu.VMEM),
        ],
        out_specs=pl.BlockSpec(memory_space=pltpu.VMEM),
        scratch_shapes=[
            pltpu.VMEM((REACH + 1, KEY_VALUE_HEADS, 2, *pair), jnp.bfloat16),
            pltpu.VMEM((KEY_VALUE_HEADS - PLUS_HEADS, 2, *pair), jnp.bfloat16),
            pltpu.VMEM(queries.shape, jnp.bfloat16),
            pltpu.VMEM((REACH + 1, 8, tokens), jnp.int32),
            pltpu.VMEM((REACH + 1, tokens, tokens), jnp.float32),
            pltpu.VMEM((KEY_VALUE_HEADS, 1, GROUP * tokens), jnp.float32),
            pltpu.VMEM((KEY_VALUE_HEADS, 1, GROUP * tokens), jnp.float32),
            pltpu.VMEM((KEY_VALUE_HEADS, HEAD_SIZE, GROUP * tokens), jnp.float32),
            pltpu.SemaphoreType.DMA((KEY_VALUE_HEADS, 2)),
            pltpu.SemaphoreType.DMA,
            pltpu.SemaphoreType.DMA(links),
            pltpu.SemaphoreType.DMA(links),
            pltpu.SemaphoreType.DMA((REACH,)),
            pltpu.SemaphoreType.DMA((REACH,)),
        ],
        compiler_params=pltpu.CompilerParams(
            collective_id=0, has_side_effects=True, vmem_limit_bytes=VMEM_BYTES
        ),
    )(*(pltpu.with_memory_space_constraint(x, pltpu.HBM) for x in (queries, keys, values)), doc_ids.reshape(1, tokens))


def solution(mesh):
    seq_size = mesh.shape["seq"]
    spec = P(("dp", "seq"), None)
    return jax.shard_map(
        functools.partial(on_device, seq_size, mesh.shape["dp"] * seq_size),
        mesh=mesh,
        in_specs=(spec, spec, spec, P(("dp", "seq"))),
        out_specs=spec,
        check_vma=False,
    )
```

time: 64.4 us -> 53.2 us (0.83)
  the two profiles are of different devices: /device:TPU:17 before, /device:TPU:1 now
where the time goes in v2:
time: 53.2 us; the launch traced here: 53 us
  Pallas kernels  51 us (96%)
  local copies, waits for them, and re-layouts  1.98 us (4%)
    pallas_call x1, Pallas kernels, on_device(): pl.pallas_call(functools.partial(kernel, seq_size, device_count, orders),...  51 us
    unnamed x3, local copies, waits for them, and re-layouts  1.98 us

profile of v2, /device:TPU:1, one launch (start us, length us, event | category | flops | bytes accessed | tf_op | source)
XLA Modules:
  0.0 53.0 jit_solution(9182491626999393803)
XLA Ops:
  0.0 0.0 copy-start
  0.0 0.7 %copy-done = s32[128]{0:T(128)S(1)} copy-done((s32[128]{0:T(128)S(1)}, s32[128]{0:T(128)}, u32[]{:S(2)}) %copy-start) | copy-done | bytes 536
  0.7 51.0 %shard_map.46 = bf16[128,8192]{1,0:T(8,128)(2,1)S(1)} custom-call(bf16[128,8192]{1,0:T(8,128)(2,1)} %queries.1, bf16[128,1024]{1,0:T(8,128)(2,1)} %keys.1, bf16[128,1024]{1,0:T(8,128)(2,1)} %values.1, s32[1,128]{1,0:T(1,128)S(1)} %bitcast.1), custom_call_target="tpu_custom_call" | custom-call | tf_op jit(solution)/shard_map/pallas_call | solution.py:187
  51.7 1.3 %copy.6 = bf16[128,8192]{1,0:T(8,128)(2,1)} copy(bf16[128,8192]{1,0:T(8,128)(2,1)S(1)} %shard_map.46) | data formatting | bytes 4194304
Async XLA Ops:
  0.0 0.7 %copy-start = (s32[128]{0:T(128)S(1)}, s32[128]{0:T(128)}, u32[]{:S(2)}) copy-start(s32[128]{0:T(128)} %param.7) | copy-start | bytes 1540

commit v3 on v2

v3 whole, which is shorter than its diff:
```python
import functools

import jax
import jax.numpy as jnp
from jax import lax
from jax.experimental import pallas as pl
from jax.experimental.pallas import tpu as pltpu
from jax.sharding import PartitionSpec as P

QUERY_HEADS = 64
KEY_VALUE_HEADS = 8
GROUP = QUERY_HEADS // KEY_VALUE_HEADS
HEAD_SIZE = 128
LONGEST_DOCUMENT = 512
VMEM_BYTES = 40 << 20
HOLD = 1
LINE = 8
TIMES = (((3.9, 1.4, 5.3), (7.0, 1.4, 4.2, 0.0), 8.0), ((3.9, 1.4, 6), (7.0, 1.4, 4.2, 3.0), 8.0))


def own_first(dp, seq):
    return lax.rem(seq, LINE) < 3


MESH = pl.DeviceIdType.MESH
SCORE_SCALE = HEAD_SIZE**-0.5 * 1.4426950408889634

ONWARD = (6, 5)
REACH = 4
PLUS, MINUS = 0, 1
STEPS = {PLUS: ((1, 2), (3, 4)), MINUS: ((4, 3), (2, 1))}
EITHER = (((4, 3), (2, 1)), ((2, 3), (1, 4)))


def sender_halves(half, distance):
    places = range(half * LINE // 2, (half + 1) * LINE // 2)
    return {(place - distance) % LINE * 2 // LINE for place in places}


def schedule(half, plus, minus, doc):
    steps = [(doc + 0.1 * distance, "doc", distance) for distance in range(1, REACH + 1)]
    for distance in range(1, REACH + 1):
        for head in range(max(ONWARD[sender] for sender in sender_halves(half, distance))):
            steps.append((plus[0] + plus[1] * ((distance - 1) * plus[2] + head), "block", PLUS, distance, head))
    for distance in range(1, REACH + 2):
        for head in range(min(ONWARD[sender] for sender in sender_halves(half, distance)), KEY_VALUE_HEADS):
            index, stage = KEY_VALUE_HEADS - 1 - head, REACH + 1 - distance
            time = minus[0] + minus[1] * index + minus[2] * stage + (minus[3] if stage else 0.0)
            steps.append((time, "block", MINUS, distance, head))
    return sorted(steps)


def kernel(
    seq_size, device_count, orders, queries, keys, values, docs, out,
    pairs, transit, query_rows, own_docs, doc_rows, bias, top, total, partial,
    local_sem, query_sem, doc_sem, send_sem, recv_sem, doc_send, doc_recv,
):
    me = lax.axis_index("dp") * seq_size + lax.axis_index("seq")

    def block_device(step):
        block = lax.rem(me + (step + device_count), device_count)
        return (block // seq_size, lax.rem(block, seq_size))

    right, left, ahead, behind = (block_device(s) for s in (1, -1, REACH + 1, -REACH - 1))
    greet = (right, left, behind, *(block_device(-distance) for distance in range(2, REACH + 1)))
    barrier = pltpu.get_barrier_semaphore()
    for device in greet:
        pl.semaphore_signal(barrier, inc=1, device_id=device, device_id_type=MESH)
    own = [pltpu.make_async_copy(docs, own_docs, doc_sem)]
    own[0].start()
    for head in reversed(range(KEY_VALUE_HEADS)):
        for part, ref in enumerate((keys, values)):
            columns = ref.at[:, pl.ds(head * HEAD_SIZE, HEAD_SIZE)]
            own.append(pltpu.make_async_copy(columns, pairs.at[0, head, part], local_sem.at[head, part]))
            own[-1].start()
    query_copy = pltpu.make_async_copy(queries, query_rows, query_sem)
    query_copy.start()
    for copy in own:
        copy.wait()
    doc_rows[0] = jnp.broadcast_to(own_docs[...], doc_rows.shape[1:])

    def remote(source, target, sent, received, device):
        return pltpu.make_async_remote_copy(
            src_ref=source, dst_ref=target, send_sem=sent, recv_sem=received, device_id=device, device_id_type=MESH
        )

    place = lax.rem(lax.axis_index("seq"), LINE)
    in_first_half = place < LINE // 2

    def by_way(half, way, distance, head, action):
        ways = {sender: PLUS if head < ONWARD[sender] else MINUS for sender in sender_halves(half, distance)}
        if set(ways.values()) == {way}:
            action()
        elif way in ways.values():
            first = lax.rem(place - distance + LINE, LINE) < LINE // 2
            pl.when(first if ways[0] == way else jnp.logical_not(first))(action)

    def block_copy(way, distance, head):
        sems = (send_sem.at[way, distance - 1, head], recv_sem.at[distance - 1, head])
        if way == PLUS:
            return remote(pairs.at[distance - 1, head], pairs.at[distance, head], *sems, right)
        if distance > REACH:
            return remote(pairs.at[0, head], transit.at[head - min(ONWARD)], *sems, ahead)
        source = transit.at[head - min(ONWARD)] if distance == REACH else pairs.at[distance + 1, head]
        return remote(source, pairs.at[distance, head], *sems, left)

    def doc_copy(distance):
        return remote(
            doc_rows.at[0], doc_rows.at[distance], doc_send.at[distance - 1], doc_recv.at[distance - 1], block_device(distance)
        )

    def attend(head, blocks, first, last):
        tokens = query_rows.shape[0]
        key_rows = jnp.concatenate([pairs[d, head, 0] for d in blocks], axis=0)
        value_rows = jnp.concatenate([pairs[d, head, 1] for d in blocks], axis=0)
        mask = jnp.concatenate([bias[d] for d in blocks], axis=0)
        columns = [pl.ds(pl.multiple_of((head * GROUP + g) * HEAD_SIZE, HEAD_SIZE), HEAD_SIZE) for g in range(GROUP)]
        rows = jnp.concatenate([query_rows[:, column] for column in columns], axis=0)
        scores = lax.dot_general(key_rows, rows, (((1,), (1,)), ((), ())), preferred_element_type=jnp.float32)
        scores = scores * SCORE_SCALE + jnp.concatenate([mask] * GROUP, axis=1)
        highest = jnp.max(scores, axis=0, keepdims=True)
        if not first:
            highest = jnp.maximum(highest, top[head])
        weight = jnp.exp2(scores - highest)
        sums = jnp.sum(weight, axis=0, keepdims=True)
        mixed = lax.dot_general(
            value_rows, weight.astype(jnp.bfloat16), (((0,), (0,)), ((), ())), preferred_element_type=jnp.float32
        )
        if not first:
            shrink = jnp.exp2(top[head] - highest)
            sums = sums + total[head] * shrink
            mixed = mixed + partial[head] * shrink
        if not last:
            top[head], total[head], partial[head] = highest, sums, mixed
            return
        mixed = mixed / sums
        for g, column in enumerate(columns):
            out[:, column] = mixed[:, g * tokens : (g + 1) * tokens].T.astype(jnp.bfloat16)

    def fill_bias(distance):
        tokens = query_rows.shape[0]
        square = (tokens, tokens)
        same = jnp.broadcast_to(doc_rows[distance, 0:1], square).T == jnp.broadcast_to(own_docs[...], square)
        if distance == 0:
            key, query = (lax.broadcasted_iota(jnp.int32, square, axis) for axis in (0, 1))
            same = same & (key <= query)
        else:
            same = same & (jnp.full(square, me, jnp.int32) >= distance)
        bias[distance] = jnp.where(same, 0.0, -jnp.inf)

    def attend_own():
        query_copy.wait()
        fill_bias(0)
        pl.loop(0, KEY_VALUE_HEADS)(lambda head: attend(head, (0,), True, False))

    early = own_first(lax.axis_index("dp"), lax.axis_index("seq"))
    pl.when(early)(attend_own)
    pl.semaphore_wait(barrier, len(greet))
    for distance in range(1, REACH + 1):
        doc_copy(distance).start()

    def send_own(half):
        for head in reversed(range(ONWARD[half], KEY_VALUE_HEADS)):
            block_copy(MINUS, REACH + 1, head).start()
        for head in range(ONWARD[half]):
            block_copy(PLUS, 1, head).start()

    pl.when(in_first_half)(lambda: send_own(0))
    pl.when(jnp.logical_not(in_first_half))(lambda: send_own(1))
    pl.when(jnp.logical_not(early))(attend_own)
    def follow(half):
        order = orders[half]
        blocks = [step[2:] for step in order if step[1] == "block"]
        work, waiting, passed = [], HOLD, set()
        unfinished = {head: [] for head in range(KEY_VALUE_HEADS)}
        for head in range(KEY_VALUE_HEADS):
            ways = {PLUS if head < onward else MINUS for onward in ONWARD}
            unfinished[head] = list(EITHER[half] if len(ways) == 2 else STEPS[ways.pop()])
        sent = [(PLUS, 1, head) for head in range(ONWARD[half])]
        sent += [(MINUS, REACH + 1, head) for head in range(ONWARD[half], KEY_VALUE_HEADS)]
        for step in order:
            if step[1] == "doc":
                doc_copy(step[2]).wait_recv()
                fill_bias(step[2])
                waiting = 0 if step[2] == REACH else waiting
                continue
            way, distance, head = step[2:]
            onward = distance + 1 if way == PLUS else distance - 1

            def arrived():
                block_copy(way, distance, head).wait_recv()
                if 1 <= onward <= REACH:
                    block_copy(way, onward, head).start()

            by_way(half, way, distance, head, arrived)
            passed.add((way, distance, head))
            for pair in list(unfinished[head]):
                if not any((w, d, head) in blocks and (w, d, head) not in passed for w in (PLUS, MINUS) for d in pair):
                    unfinished[head].remove(pair)
                    work.append((head, pair, False, not unfinished[head]))
            if work and not waiting:
                attend(*work.pop(0))
        for item in work:
            attend(*item)
        for copy in sent:
            block_copy(*copy).wait_send()
        for way, distance, head in blocks:
            onward = distance + 1 if way == PLUS else distance - 1
            if 1 <= onward <= REACH:
                by_way(half, way, distance, head, lambda: block_copy(way, onward, head).wait_send())

    pl.when(in_first_half)(lambda: follow(0))
    pl.when(jnp.logical_not(in_first_half))(lambda: follow(1))
    for distance in range(1, REACH + 1):
        doc_copy(distance).wait_send()


def on_device(seq_size, device_count, queries, keys, values, doc_ids):
    tokens = queries.shape[0]
    orders = [schedule(half, *times) for half, times in enumerate(TIMES)]
    pair = (tokens, HEAD_SIZE)
    links = (REACH + 1, KEY_VALUE_HEADS)
    return pl.pallas_call(
        functools.partial(kernel, seq_size, device_count, orders),
        out_shape=jax.ShapeDtypeStruct(queries.shape, jnp.bfloat16),
        in_specs=[
            pl.BlockSpec(memory_space=pltpu.HBM),
            pl.BlockSpec(memory_space=pltpu.HBM),
            pl.BlockSpec(memory_space=pltpu.HBM),
            pl.BlockSpec(memory_space=pltpu.HBM),
        ],
        out_specs=pl.BlockSpec(memory_space=pltpu.VMEM),
        scratch_shapes=[
            pltpu.VMEM((REACH + 1, KEY_VALUE_HEADS, 2, *pair), jnp.bfloat16),
            pltpu.VMEM((KEY_VALUE_HEADS - min(ONWARD), 2, *pair), jnp.bfloat16),
            pltpu.VMEM(queries.shape, jnp.bfloat16),
            pltpu.VMEM((1, tokens), jnp.int32),
            pltpu.VMEM((REACH + 1, 8, tokens), jnp.int32),
            pltpu.VMEM((REACH + 1, tokens, tokens), jnp.float32),
            pltpu.VMEM((KEY_VALUE_HEADS, 1, GROUP * tokens), jnp.float32),
            pltpu.VMEM((KEY_VALUE_HEADS, 1, GROUP * tokens), jnp.float32),
            pltpu.VMEM((KEY_VALUE_HEADS, HEAD_SIZE, GROUP * tokens), jnp.float32),
            pltpu.SemaphoreType.DMA((KEY_VALUE_HEADS, 2)),
            pltpu.SemaphoreType.DMA,
            pltpu.SemaphoreType.DMA,
            pltpu.SemaphoreType.DMA((2, *links)),
            pltpu.SemaphoreType.DMA(links),
            pltpu.SemaphoreType.DMA((REACH,)),
            pltpu.SemaphoreType.DMA((REACH,)),
        ],
        compiler_params=pltpu.CompilerParams(
            collective_id=0, has_side_effects=True, vmem_limit_bytes=VMEM_BYTES
        ),
    )(*(pltpu.with_memory_space_constraint(x, pltpu.HBM) for x in (queries, keys, values, doc_ids.reshape(1, tokens))))


def solution(mesh):
    seq_size = mesh.shape["seq"]
    spec = P(("dp", "seq"), None)
    return jax.shard_map(
        functools.partial(on_device, seq_size, mesh.shape["dp"] * seq_size),
        mesh=mesh,
        in_specs=(spec, spec, spec, P(("dp", "seq"))),
        out_specs=spec,
        check_vma=False,
    )
```

time: 53.2 us -> 51.8 us (0.974)
  Pallas kernels: 51 us -> 50.3 us
  local copies, waits for them, and re-layouts: 1.98 us -> 1.32 us
    pallas_call x1, Pallas kernels: 51 us -> 50.3 us  [on_device(): pl.pallas_call(functools.partial(kernel, seq_size, device_count, orders),...]
    unnamed x3 -> x1, local copies, waits for them, and re-layouts: 1.98 us -> 1.32 us
where the time goes in v3:
time: 51.8 us; the launch traced here: 51.6 us
  Pallas kernels  50.3 us (97%)
  local copies, waits for them, and re-layouts  1.32 us (3%)
    pallas_call x1, Pallas kernels, on_device(): pl.pallas_call(functools.partial(kernel, seq_size, device_count, orders),...  50.3 us
    unnamed x1, local copies, waits for them, and re-layouts  1.32 us

profile of v3, /device:TPU:1, one launch (start us, length us, event | category | flops | bytes accessed | tf_op | source)
XLA Modules:
  0.0 51.6 jit_solution(11601200561307788331)
XLA Ops:
  0.0 50.3 %shard_map.46 = bf16[128,8192]{1,0:T(8,128)(2,1)S(1)} custom-call(bf16[128,8192]{1,0:T(8,128)(2,1)} %queries.1, bf16[128,1024]{1,0:T(8,128)(2,1)} %keys.1, bf16[128,1024]{1,0:T(8,128)(2,1)} %values.1, s32[1,128]{1,0:T(1,128)} %bitcast.1), custom_call_target="tpu_custom_call" | custom-call | tf_op jit(solution)/shard_map/pallas_call | solution.py:223
  50.3 1.3 %copy.6 = bf16[128,8192]{1,0:T(8,128)(2,1)} copy(bf16[128,8192]{1,0:T(8,128)(2,1)S(1)} %shard_map.46) | data formatting | bytes 4194304

commit v4 on v3

--- a/solution.py
+++ b/solution.py
@@ -68,15 +68,16 @@
         pl.semaphore_signal(barrier, inc=1, device_id=device, device_id_type=MESH)
     own = [pltpu.make_async_copy(docs, own_docs, doc_sem)]
     own[0].start()
-    for head in reversed(range(KEY_VALUE_HEADS)):
+    landing = {}
+    for head in (*reversed(range(min(ONWARD), KEY_VALUE_HEADS)), *range(min(ONWARD))):
         for part, ref in enumerate((keys, values)):
             columns = ref.at[:, pl.ds(head * HEAD_SIZE, HEAD_SIZE)]
             own.append(pltpu.make_async_copy(columns, pairs.at[0, head, part], local_sem.at[head, part]))
             own[-1].start()
+            landing.setdefault(head, []).append(own[-1])
     query_copy = pltpu.make_async_copy(queries, query_rows, query_sem)
     query_copy.start()
-    for copy in own:
-        copy.wait()
+    own.pop(0).wait()
     doc_rows[0] = jnp.broadcast_to(own_docs[...], doc_rows.shape[1:])
 
     def remote(source, target, sent, received, device):
@@ -153,6 +154,12 @@
         fill_bias(0)
         pl.loop(0, KEY_VALUE_HEADS)(lambda head: attend(head, (0,), True, False))
 
+    def wait_own(heads):
+        for head in heads:
+            for copy in landing[head]:
+                copy.wait()
+
+    pl.when(in_first_half)(lambda: wait_own(range(KEY_VALUE_HEADS)))
     early = own_first(lax.axis_index("dp"), lax.axis_index("seq"))
     pl.when(early)(attend_own)
     pl.semaphore_wait(barrier, len(greet))
@@ -161,8 +168,12 @@
 
     def send_own(half):
         for head in reversed(range(ONWARD[half], KEY_VALUE_HEADS)):
+            if half == 1:
+                wait_own([head])
             block_copy(MINUS, REACH + 1, head).start()
         for head in range(ONWARD[half]):
+            if half == 1:
+                wait_own([head])
             block_copy(PLUS, 1, head).start()
 
     pl.when(in_first_half)(lambda: send_own(0))

time: 51.8 us -> 52.1 us (level)
  no operation moved by 1% of the time
where the time goes in v4:
time: 52.1 us; the launch traced here: 51.9 us
  Pallas kernels  50.6 us (97%)
  local copies, waits for them, and re-layouts  1.32 us (3%)
    pallas_call x1, Pallas kernels, on_device(): pl.pallas_call(functools.partial(kernel, seq_size, device_count, orders),...  50.6 us
    unnamed x1, local copies, waits for them, and re-layouts  1.32 us

profile of v4, /device:TPU:1, one launch (start us, length us, event | category | flops | bytes accessed | tf_op | source)
XLA Modules:
  0.0 51.9 jit_solution(13118719879605112054)
XLA Ops:
  0.0 50.6 %shard_map.46 = bf16[128,8192]{1,0:T(8,128)(2,1)S(1)} custom-call(bf16[128,8192]{1,0:T(8,128)(2,1)} %queries.1, bf16[128,1024]{1,0:T(8,128)(2,1)} %keys.1, bf16[128,1024]{1,0:T(8,128)(2,1)} %values.1, s32[1,128]{1,0:T(1,128)} %bitcast.1), custom_call_target="tpu_custom_call" | custom-call | tf_op jit(solution)/shard_map/pallas_call | solution.py:234
  50.6 1.3 %copy.6 = bf16[128,8192]{1,0:T(8,128)(2,1)} copy(bf16[128,8192]{1,0:T(8,128)(2,1)S(1)} %shard_map.46) | data formatting | bytes 4194304
